TPU v7x, 128 devices: a whole 4x4x4 slice. The times are simulated.
128 devices in a mesh: rep: 2 (over y_lo), tx: 8 (over x, y_hi), ty: 8 (over z, core).
Axes of the slice: x: 4, y: 4 (y_hi: 2, y_lo: 2; y = y_hi * 2 + y_lo), z: 4, core: 2. Of those that a mesh axis runs over, the one named last changes fastest.
Arguments:
- density: bfloat16 [2, 256, 512, 128], P('rep', 'tx', 'ty'), may hold values from -6 to 6
- kernel_one: bfloat16 [16, 4, 3, 3, 3], replicated, may hold values from -0.625 to 0.625
- kernel_two: bfloat16 [16, 16, 3, 3, 3], replicated, may hold values from -0.3125 to 0.3125
- cotangent: bfloat16 [2, 128, 256, 256], P('rep', 'tx', 'ty'), may hold values from -30 to 30
Outputs:
- features: bfloat16 [2, 128, 256, 256], P('rep', 'tx', 'ty')
- grad_one: float32 [16, 4, 3, 3, 3], replicated
- grad_two: float32 [16, 16, 3, 3, 3], replicated
All inputs are finite; a program needn't handle non-finite values.
Results may differ from a plain program's by a relative error of at most 0.015.
Values may be sent and summed in bfloat16 or wider, within the bound.
No kernel may reach another device: no remote copies, remote signals or barrier semaphores. Data moves between devices by JAX's collectives and lax.ppermute only.
A program may use at most 320 MiB of HBM per device.

v0:
```python
import jax
import jax.numpy as jnp
from jax import lax
from jax.sharding import PartitionSpec as P

CIN = 4
CH = 16
leak_slope = 0.3


def extended(value, sides, width):
    for axis, dim in sides:
        peers, length = (lax.axis_size(axis), value.shape[dim])
        up = [(i, (i + 1) % peers) for i in range(peers)]
        down = [(j, i) for i, j in up]
        last = lax.slice_in_dim(value, length - width, length, axis=dim)
        initial = lax.slice_in_dim(value, 0, width, axis=dim)
        before = lax.ppermute(last, axis, up)
        after = lax.ppermute(initial, axis, down)
        value = jnp.concatenate([before, value, after], axis=dim)
    return value


def convolve(lhs, rhs, specs):
    return lax.conv_general_dilated(
        lhs, rhs, (1, 1, 1), "VALID", dimension_numbers=specs, preferred_element_type=jnp.float32
    )


def depth_pad(field):
    return jnp.pad(field, ((0, 0), (0, 0), (1, 1), (0, 0), (0, 0)))


def pooling(field):
    s, c, d, x, y = field.shape
    blocks = field.astype(jnp.float32).reshape(s, c, d // 2, 2, x // 2, 2, y // 2, 2)
    return jnp.mean(blocks, axis=(3, 5, 7))


def upsample(field):
    s, c, d, x, y = field.shape
    grown = jnp.broadcast_to(field[:, :, :, None, :, None, :, None], (s, c, d, 2, x, 2, y, 2))
    return grown.reshape(s, c, 2 * d, 2 * x, 2 * y)


def unpack(field, channels):
    s, x, y, merged = field.shape
    return jnp.transpose(field.reshape(s, x, y, channels, merged // channels), (0, 3, 4, 1, 2))


def packing(field):
    s, c, d, x, y = field.shape
    return jnp.transpose(field, (0, 3, 4, 1, 2)).reshape(s, x, y, c * d)


def on_device(density, kernel_one, kernel_two, cotangent):
    forward = ("NCDHW", "OIDHW", "NCDHW")
    weight_form = ("CNDHW", "IODHW", "CNDHW")
    backward = ("NCDHW", "IODHW", "NCDHW")
    fine_width = 1
    grads = unpack(cotangent, CH)
    wide = unpack(extended(density, (("tx", 1), ("ty", 2)), fine_width), CIN)
    grad_rim = unpack(extended(cotangent, (("tx", 1), ("ty", 2)), 1), CH)
    padded = depth_pad(wide)
    pre = convolve(padded, kernel_one, forward)
    act = jnp.where(pre > 0, pre, leak_slope * pre).astype(jnp.bfloat16)
    pooled = pooling(act).astype(jnp.bfloat16)
    pooled_rimmed = extended(packing(pooled), (("tx", 1), ("ty", 2)), 1)
    pooled_pad = depth_pad(unpack(pooled_rimmed, CH))
    features = packing(convolve(pooled_pad, kernel_two, forward).astype(jnp.bfloat16))
    slab_two = convolve(pooled_pad, grads, weight_form)
    grad_pad = depth_pad(grad_rim)
    flipped = kernel_two[:, :, ::-1, ::-1, ::-1]
    back_pooled = convolve(grad_pad, flipped, backward).astype(jnp.bfloat16)
    slope = jnp.where(pre > 0, 1.0, leak_slope).astype(jnp.float32)
    back_pre = (upsample(back_pooled.astype(jnp.float32)) * 0.125 * slope).astype(jnp.bfloat16)
    slab_one = convolve(padded, back_pre, weight_form)
    replicas = lax.axis_size("rep")
    tile_one, tile_two = lax.psum((slab_one, slab_two), ("tx", "ty"))
    total_one, total_two = (
        lax.psum(tile_one.astype(jnp.bfloat16), "rep").astype(jnp.float32),
        lax.psum(tile_two.astype(jnp.bfloat16), "rep").astype(jnp.float32),
    )
    return (features, total_one / replicas, total_two / replicas)


def solution(mesh):
    in_specs = (P("rep", "tx", "ty", None), P(), P(), P("rep", "tx", "ty", None))
    out_specs = (P("rep", "tx", "ty", None), P(), P())
    return jax.shard_map(
        on_device, mesh=mesh, in_specs=in_specs, out_specs=out_specs, check_vma=False
    )
```

profile of v0, /device:TPU:0, one launch (start us, length us, event | category | flops | bytes accessed | tf_op | source)
XLA Modules:
  0.0 1262.0 jit_solution(5296581193335295249)
XLA Ops:
  0.6 1.6 copy.191
  2.2 3.3 collective-permute-start
  5.6 2.4 collective-permute-start.1
  8.7 3.4 collective-permute-start.9
  13.6 7.6 copy.227
  23.9 2.6 collective-permute-start.3
  28.0 2.4 copy.215
  31.6 3.0 collective-permute-start.11
  35.2 1.5 copy.197
  36.7 2.4 pad_maximum_fusion.4
  39.0 4.1 copy.233
  44.7 15.7 %copy.199 = bf16[34,1,8,11,4,32]{2,4,3,0,5,1:T(4,128)(2,1)} copy(bf16[34,1,8,11,4,32]{0,5,4,3,2,1:T(8,128)(2,1)S(1)} %fusion.23) | data formatting | bytes 1531904 | tf_op jit(solution)/shard_map/conv_general_dilated | solution.py:25
  60.4 79.3 %fusion.4 = f32[32,32,8,9,16]{4,2,3,1,0:T(8,128)} fusion(bf16[16,4,3,3,3]{0,1,4,3,2:T(4,128)(2,1)S(1)} %copy-done.13, bf16[34,1,8,11,4,32]{2,4,3,0,5,1:T(4,128)(2,1)} %copy.199), kind=kOutput, calls=%fused_computation.8 | convolution fusion | flops 249495552 | bytes 5488000 | tf_op jit(solution)/shard_map/conv_general_dilated | solution.py:25
  139.7 27.7 %copy.200 = f32[32,32,8,9,16]{1,4,3,2,0:T(8,128)} copy(f32[32,32,8,9,16]{4,2,3,1,0:T(8,128)} %fusion.4) | data formatting | bytes 9437184 | tf_op jit(solution)/shard_map/conv_general_dilated | solution.py:25
  167.4 17.8 %compare_select_fusion = (f32[32,32,8,9,16]{1,4,3,2,0:T(8,128)}, bf16[32,32,8,9,16]{1,4,3,2,0:T(8,128)(2,1)}) fusion(f32[32,32,8,9,16]{1,4,3,2,0:T(8,128)} %copy.200, pred[8,9]{1,0:T(8,128)(4,1)S(1)} %copy-done.12), kind=kLoop, calls=%fused_computation.5 | loop fusion | flops 7077888 | bytes 11796552 | tf_op jit(solution)/shard_map/jit(_where)/select_n | solution.py:75
  185.2 11.3 convert_bitcast_fusion
  196.5 30.0 %copy.201 = f32[1,16,32,32,64]{1,4,3,2,0:T(8,128)} copy(f32[1,16,32,32,64]{3,1,4,2,0:T(8,128)} %convert_bitcast_fusion) | data formatting | bytes 8388608 | tf_op jit(solution)/shard_map/reshape | solution.py:36
  226.5 25.2 %reduce_sum.9 = f32[16,16,16,32]{0,3,2,1:T(8,128)} reduce(f32[16,16,2,16,2,32,2]{0,6,5,4,3,2,1:T(2,128)} %bitcast.52, f32[]{:T(128)} %constant.5.clone.1), dimensions={2,4,6}, to_apply=%region_0.1 | reduce | flops 917504 | bytes 4718596 | tf_op jit(solution)/shard_map/reduce_sum | solution.py:37
  251.7 2.7 fusion.24
  255.6 11.7 slice.71
  267.3 1.9 collective-permute-start.4
  269.2 3.8 collective-permute-start.5
  273.0 30.0 %copy.232 = f32[32,32,1,64,16]{4,3,1,0,2:T(8,128)} copy(f32[32,32,1,64,16]{1,4,3,0,2:T(8,128)} %slice.71) | data formatting | bytes 8388608
  302.9 65.3 %copy.223 = bf16[1,34,66,4,32]{3,0,2,1,4:T(2,128)(2,1)} copy(bf16[1,34,66,4,32]{2,4,3,1,0:T(8,128)(2,1)S(1)} %bitcast.67) | data formatting | bytes 1148928 | tf_op jit(solution)/shard_map/reshape | solution.py:48
  369.7 2.2 copy.216
  371.8 3.5 pad_maximum_fusion.2
  375.3 6.2 copy.234
  381.6 2.3 pad.9.clone
  383.8 5.9 copy.219
  389.7 1.6 slice.69
  391.4 7.8 convert_multiply_fusion
  401.7 16.6 %broadcast_in_dim.12 = f32[16,16,2,16,2,32,2]{0,6,5,4,3,2,1:T(2,128)} broadcast(f32[16,16,16,32]{0,3,2,1:T(8,128)S(1)} %copy.221), dimensions={0,1,3,5} | broadcast | bytes 4718592 | tf_op jit(solution)/shard_map/broadcast_in_dim | solution.py:42
  418.3 27.8 %fusion = bf16[1,16,32,32,64]{1,4,3,2,0:T(8,128)(2,1)} fusion(f32[1,16,32,32,64]{1,4,3,2,0:T(8,128)} %bitcast.53, f32[32,32,1,64,16]{4,3,1,0,2:T(8,128)} %copy.232), kind=kLoop, calls=%fused_computation.1 | loop fusion | flops 2097152 | bytes 10485760 | tf_op jit(solution)/shard_map/convert_element_type | solution.py:76
  449.3 2.4 collective-permute-start.7
  451.7 374.3 %fusion.1 = f32[16,4,3,3,3]{0,1,4,3,2:T(4,128)} fusion(bf16[1,34,66,4,32]{3,0,2,1,4:T(2,128)(2,1)} %copy.223, bf16[1,16,32,32,64]{1,4,3,2,0:T(8,128)(2,1)} %fusion), kind=kOutput, calls=%fused_computation.2 | convolution fusion | flops 221773824 | bytes 2678528 | tf_op jit(solution)/shard_map/conv_general_dilated | solution.py:25
  827.4 2.2 copy.206
  829.7 2.4 pad_maximum_fusion.1
  832.1 5.2 copy.207
  837.3 2.2 pad.7
  839.4 7.2 copy.209
  846.7 1.6 slice.65
  848.3 7.6 select_convert_fusion.1
  856.9 2.9 copy.211
  859.8 2.2 copy.228
  862.0 9.7 copy.226
  871.7 48.2 %fusion.43 = f32[16,16,3,3,3]{0,1,4,3,2:T(8,128)S(1)} fusion(bf16[1,18,34,16,16]{3,0,2,1,4:T(2,128)(2,1)} %copy.226, bf16[1,16,32,16,16]{3,0,2,1,4:T(2,128)(2,1)} %copy.227), kind=kOutput, calls=%fused_computation.59 | convolution fusion | flops 108527616 | bytes 603136 | tf_op jit(solution)/shard_map/conv_general_dilated | solution.py:25
  920.0 331.5 %all-reduce = (bf16[16,4,3,3,3]{0,1,4,3,2:T(4,128)(2,1)S(1)}, bf16[16,16,3,3,3]{0,1,4,3,2:T(8,128)(2,1)S(1)}) all-reduce(f32[16,4,3,3,3]{0,1,4,3,2:T(4,128)S(1)} %copy-done.11, f32[16,16,3,3,3]{0,1,4,3,2:T(8,128)S(1)} %fusion.43), channel_id=1, replica_groups=mesh['rep'=2,'tx'=8,'ty'=8] {'tx','ty'}, use_global_device_ids=true, to_apply=%region_1.2 | all-reduce | flops 8640 | bytes 51840 | tf_op jit(solution)/shard_map/psum | solution.py:79
  1251.5 8.8 all-reduce.1
  (81 shorter events, 22.0 us)
Async XLA Ops:
  0.6 390.7 %copy-start = (bf16[16,16,3,3,3]{1,0,4,3,2:T(8,128)(2,1)S(1)}, bf16[16,16,3,3,3]{1,0,4,3,2:T(8,128)(2,1)}, u32[]{:S(2)}) copy-start(bf16[16,16,3,3,3]{1,0,4,3,2:T(8,128)(2,1)} %param.6) | copy-start | bytes 41476
  2.2 19.0 %collective-permute-start = (bf16[1,1,64,128]{2,3,1,0:T(8,128)(2,1)S(1)}, bf16[1,1,64,128]{2,3,1,0:T(8,128)(2,1)S(1)}, u32[]{:S(2)}, u32[]{:S(2)}) collective-permute-start(bf16[1,1,64,128]{2,3,1,0:T(8,128)(2,1)S(1)} %get-tuple-element.36), channel_id=1, source_target_pairs={{0,8},{8,16},{16,24},{24,32},{32,40},{40,48},{48,56},{56,0},{1,9},... | collective-permute-start | bytes 49160 | tf_op jit(solution)/shard_map/ppermute | solution.py:18
  5.6 15.7 %collective-permute-start.1 = (bf16[1,1,64,128]{2,3,1,0:T(8,128)(2,1)S(1)}, bf16[1,1,64,128]{2,3,1,0:T(8,128)(2,1)S(1)}, u32[]{:S(2)}, u32[]{:S(2)}) collective-permute-start(bf16[1,1,64,128]{2,3,1,0:T(8,128)(2,1)S(1)} %get-tuple-element.37), channel_id=1, source_target_pairs={{8,0},{16,8},{24,16},{32,24},{40,32},{48,40},{56,48},{0,56},{9,1},... | collective-permute-start | bytes 49160 | tf_op jit(solution)/shard_map/ppermute | solution.py:19
  8.7 17.8 %collective-permute-start.9 = (bf16[1,1,32,256]{3,2,1,0:T(8,128)(2,1)S(1)}, bf16[1,1,32,256]{3,2,1,0:T(8,128)(2,1)S(1)}, u32[]{:S(2)}, u32[]{:S(2)}) collective-permute-start(bf16[1,1,32,256]{3,2,1,0:T(8,128)(2,1)S(1)} %get-tuple-element.40), channel_id=1, source_target_pairs={{8,0},{16,8},{24,16},{32,24},{40,32},{48,40},{56,48},{0,56},{9,1},... | collective-permute-start | bytes 49160 | tf_op jit(solution)/shard_map/ppermute | solution.py:19
  12.0 10.0 collective-permute-start.8
  21.2 0.9 copy-start.7
  22.2 0.7 copy-start.8
  23.9 11.3 collective-permute-start.3
  26.4 8.1 collective-permute-start.2
  31.6 338.1 %collective-permute-start.11 = (bf16[1,18,1,256]{3,1,2,0:T(8,128)(2,1)}, bf16[1,18,1,256]{3,1,2,0:T(8,128)(2,1)}, u32[]{:S(2)}, u32[]{:S(2)}) collective-permute-start(bf16[1,18,1,256]{3,1,2,0:T(8,128)(2,1)} %copy.231), channel_id=1, source_target_pairs={{1,0},{2,1},{3,2},{4,3},{5,4},{6,5},{7,6},{0,7},{9,8},{10,9},{11,1... | collective-permute-start | bytes 27656 | tf_op jit(solution)/shard_map/ppermute | solution.py:19
  34.5 333.7 %collective-permute-start.10 = (bf16[1,18,1,256]{3,1,2,0:T(8,128)(2,1)}, bf16[1,18,1,256]{3,1,2,0:T(8,128)(2,1)}, u32[]{:S(2)}, u32[]{:S(2)}) collective-permute-start(bf16[1,18,1,256]{3,1,2,0:T(8,128)(2,1)} %copy.230), channel_id=1, source_target_pairs={{0,1},{1,2},{2,3},{3,4},{4,5},{5,6},{6,7},{7,0},{8,9},{9,10},{10,1... | collective-permute-start | bytes 27656 | tf_op jit(solution)/shard_map/ppermute | solution.py:18
  39.0 4.8 copy-start.4
  44.7 15.7 %copy-start.13 = (bf16[16,4,3,3,3]{0,1,4,3,2:T(4,128)(2,1)S(1)}, bf16[16,4,3,3,3]{0,1,4,3,2:T(4,128)(2,1)}, u32[]{:S(2)}) copy-start(bf16[16,4,3,3,3]{0,1,4,3,2:T(4,128)(2,1)} %param.5) | copy-start | bytes 10372
  139.7 27.7 %copy-start.12 = (pred[8,9]{1,0:T(8,128)(4,1)S(1)}, pred[8,9]{1,0:T(8,128)(4,1)}, u32[]{:S(2)}) copy-start(pred[8,9]{1,0:T(8,128)(4,1)} %constant.34) | copy-start | bytes 220
  255.6 11.7 copy-start.1
  267.3 178.8 %collective-permute-start.4 = (bf16[1,1,32,256]{2,3,1,0:T(8,128)(2,1)S(1)}, bf16[1,1,32,256]{2,3,1,0:T(8,128)(2,1)S(1)}, u32[]{:S(2)}, u32[]{:S(2)}) collective-permute-start(bf16[1,1,32,256]{2,3,1,0:T(8,128)(2,1)S(1)} %get-tuple-element.34), channel_id=1, source_target_pairs={{0,8},{8,16},{16,24},{24,32},{32,40},{40,48},{48,56},{56,0},{1,9},... | collective-permute-start | bytes 49160 | tf_op jit(solution)/shard_map/ppermute | solution.py:18
  269.2 33.7 %copy-start.5 = (bf16[1,34,66,128]{2,3,1,0:T(8,128)(2,1)S(1)}, bf16[1,34,66,128]{2,3,1,0:T(8,128)(2,1)}, u32[]{:S(2)}) copy-start(bf16[1,34,66,128]{2,3,1,0:T(8,128)(2,1)} %copy-done.4) | copy-start | bytes 1723396
  269.2 176.9 %collective-permute-start.5 = (bf16[1,1,32,256]{2,3,1,0:T(8,128)(2,1)S(1)}, bf16[1,1,32,256]{2,3,1,0:T(8,128)(2,1)S(1)}, u32[]{:S(2)}, u32[]{:S(2)}) collective-permute-start(bf16[1,1,32,256]{2,3,1,0:T(8,128)(2,1)S(1)} %get-tuple-element.35), channel_id=1, source_target_pairs={{8,0},{16,8},{24,16},{32,24},{40,32},{48,40},{56,48},{0,56},{9,1},... | collective-permute-start | bytes 49160 | tf_op jit(solution)/shard_map/ppermute | solution.py:19
  368.2 3.6 copy-start.6
  383.8 7.6 copy-start.14
  418.3 27.8 %copy-start.2 = (bf16[1,16,32,16,16]{2,4,3,1,0:T(8,128)(2,1)S(1)}, bf16[1,16,32,16,16]{2,4,3,1,0:T(8,128)(2,1)}, u32[]{:S(2)}) copy-start(bf16[1,16,32,16,16]{2,4,3,1,0:T(8,128)(2,1)} %copy-done.1) | copy-start | bytes 786436
  446.1 0.8 copy-start.9
  446.1 0.8 copy-start.10
  449.3 378.2 %collective-permute-start.7 = (bf16[1,18,1,256]{3,1,2,0:T(8,128)(2,1)}, bf16[1,18,1,256]{3,1,2,0:T(8,128)(2,1)}, u32[]{:S(2)}, u32[]{:S(2)}) collective-permute-start(bf16[1,18,1,256]{3,1,2,0:T(8,128)(2,1)} %copy.204), channel_id=1, source_target_pairs={{1,0},{2,1},{3,2},{4,3},{5,4},{6,5},{7,6},{0,7},{9,8},{10,9},{11,1... | collective-permute-start | bytes 27656 | tf_op jit(solution)/shard_map/ppermute | solution.py:19
  451.7 374.3 %collective-permute-start.6 = (bf16[1,18,1,256]{3,1,2,0:T(8,128)(2,1)}, bf16[1,18,1,256]{3,1,2,0:T(8,128)(2,1)}, u32[]{:S(2)}, u32[]{:S(2)}) collective-permute-start(bf16[1,18,1,256]{3,1,2,0:T(8,128)(2,1)} %copy.203), channel_id=1, source_target_pairs={{0,1},{1,2},{2,3},{3,4},{4,5},{5,6},{6,7},{7,0},{8,9},{9,10},{10,1... | collective-permute-start | bytes 27656 | tf_op jit(solution)/shard_map/ppermute | solution.py:18
  826.0 3.7 copy-start.3
  839.4 8.9 copy-start.15
  871.7 48.2 %copy-start.11 = (f32[16,4,3,3,3]{0,1,4,3,2:T(4,128)S(1)}, f32[16,4,3,3,3]{0,1,4,3,2:T(4,128)}, u32[]{:S(2)}) copy-start(f32[16,4,3,3,3]{0,1,4,3,2:T(4,128)} %fusion.1) | copy-start | bytes 20740
where the time goes:
time: 1270 us; the launch traced here: 1260 us
  matrix products  517 us (41%)
  blocking collectives  340 us (27%)
  local copies, waits for them, and re-layouts  285 us (22%)
  other arithmetic  95 us (7%)
  starting transfers between devices  22.8 us (2%)
    conv_general_dilated x5, matrix products, convolve(): lax.conv_general_dilated(lhs, rhs, (1, 1, 1), 'VALID', dimension_numbers=...  517 us
    psum x1, blocking collectives, on_device(): tile_one, tile_two = lax.psum((slab_one, slab_two), ('tx', 'ty'))  332 us
    reshape x7, local copies, waits for them, and re-layouts, unpack(): field.reshape(s, x, y, channels, merged // channels)  92.8 us
    conv_general_dilated x7, local copies, waits for them, and re-layouts, convolve(): lax.conv_general_dilated(lhs, rhs, (1, 1, 1), 'VALID', dimension_numbers=...  59.8 us
    unnamed x43, local copies, waits for them, and re-layouts  48.5 us
    reshape x1, local copies, waits for them, and re-layouts, pooling(): field.astype(jnp.float32).reshape(s, c, d // 2, 2, x // 2, 2, y // 2, 2)  30 us
    convert_element_type x1, other arithmetic, on_device(): (upsample(back_pooled.astype(jnp.float32)) * 0.125 * slope).astype(jnp.bf...  27.8 us
  transfers between devices with their start and end apart: 12, of which 0 were waited for; matrix products, arithmetic and copies ran while one was open for 63% of the time, Pallas kernels for 0%

commit v1 on v0

--- a/solution.py
+++ b/solution.py
@@ -76,7 +76,7 @@
     back_pre = (upsample(back_pooled.astype(jnp.float32)) * 0.125 * slope).astype(jnp.bfloat16)
     slab_one = convolve(padded, back_pre, weight_form)
     replicas = lax.axis_size("rep")
-    tile_one, tile_two = lax.psum((slab_one, slab_two), ("tx", "ty"))
+    tile_one, tile_two = lax.psum(lax.psum((slab_one, slab_two), "ty"), "tx")
     total_one, total_two = (
         lax.psum(tile_one.astype(jnp.bfloat16), "rep").astype(jnp.float32),
         lax.psum(tile_two.astype(jnp.bfloat16), "rep").astype(jnp.float32),

time: 1270 us -> 1010 us (0.80)
  blocking collectives: 340 us -> 81.6 us
    psum x1 -> x2, blocking collectives: 332 us -> 72.4 us  [on_device(): tile_one, tile_two = lax.psum(lax.psum((slab_one, slab_two), 'ty'), 'tx')]
  transfers between devices with their start and end apart: 12 -> 12, of which waited for: 0 -> 0; matrix products, arithmetic and copies ran while one was open for 63% -> 80% of each run, Pallas kernels for 0% -> 0%
where the time goes in v1:
time: 1010 us; the launch traced here: 1000 us
  matrix products  517 us (51%)
  local copies, waits for them, and re-layouts  285 us (28%)
  other arithmetic  94.9 us (9%)
  blocking collectives  81.6 us (8%)
  starting transfers between devices  22.8 us (2%)
    conv_general_dilated x5, matrix products, convolve(): lax.conv_general_dilated(lhs, rhs, (1, 1, 1), 'VALID', dimension_numbers=...  517 us
    reshape x7, local copies, waits for them, and re-layouts, unpack(): field.reshape(s, x, y, channels, merged // channels)  92.7 us
    psum x2, blocking collectives, on_device(): tile_one, tile_two = lax.psum(lax.psum((slab_one, slab_two), 'ty'), 'tx')  72.4 us
    conv_general_dilated x7, local copies, waits for them, and re-layouts, convolve(): lax.conv_general_dilated(lhs, rhs, (1, 1, 1), 'VALID', dimension_numbers=...  59.8 us
    unnamed x43, local copies, waits for them, and re-layouts  48.5 us
    reshape x1, local copies, waits for them, and re-layouts, pooling(): field.astype(jnp.float32).reshape(s, c, d // 2, 2, x // 2, 2, y // 2, 2)  30 us
    convert_element_type x1, other arithmetic, on_device(): (upsample(back_pooled.astype(jnp.float32)) * 0.125 * slope).astype(jnp.bf...  27.8 us
    reduce_sum x1, other arithmetic, pooling(): return jnp.mean(blocks, axis=(3, 5, 7))  25.2 us
  transfers between devices with their start and end apart: 12, of which 0 were waited for; matrix products, arithmetic and copies ran while one was open for 80% of the time, Pallas kernels for 0%

profile of v1, /device:TPU:0, one launch (start us, length us, event | category | flops | bytes accessed | tf_op | source)
XLA Modules:
  0.0 1003.1 jit_solution(9812793434378419840)
XLA Ops:
  0.6 1.6 copy.191
  2.2 3.3 collective-permute-start
  5.6 2.4 collective-permute-start.1
  8.7 3.4 collective-permute-start.9
  13.6 7.5 copy.227
  23.8 2.6 collective-permute-start.3
  27.9 2.4 copy.215
  31.5 3.0 collective-permute-start.11
  36.6 2.4 pad_maximum_fusion.4
  39.0 4.1 copy.233
  44.6 15.7 %copy.199 = bf16[34,1,8,11,4,32]{2,4,3,0,5,1:T(4,128)(2,1)} copy(bf16[34,1,8,11,4,32]{0,5,4,3,2,1:T(8,128)(2,1)S(1)} %fusion.23) | data formatting | bytes 1531904 | tf_op jit(solution)/shard_map/conv_general_dilated | solution.py:25
  60.3 79.3 %fusion.4 = f32[32,32,8,9,16]{4,2,3,1,0:T(8,128)} fusion(bf16[16,4,3,3,3]{0,1,4,3,2:T(4,128)(2,1)S(1)} %copy-done.13, bf16[34,1,8,11,4,32]{2,4,3,0,5,1:T(4,128)(2,1)} %copy.199), kind=kOutput, calls=%fused_computation.8 | convolution fusion | flops 249495552 | bytes 5488000 | tf_op jit(solution)/shard_map/conv_general_dilated | solution.py:25
  139.6 27.7 %copy.200 = f32[32,32,8,9,16]{1,4,3,2,0:T(8,128)} copy(f32[32,32,8,9,16]{4,2,3,1,0:T(8,128)} %fusion.4) | data formatting | bytes 9437184 | tf_op jit(solution)/shard_map/conv_general_dilated | solution.py:25
  167.3 17.7 %compare_select_fusion = (f32[32,32,8,9,16]{1,4,3,2,0:T(8,128)}, bf16[32,32,8,9,16]{1,4,3,2,0:T(8,128)(2,1)}) fusion(f32[32,32,8,9,16]{1,4,3,2,0:T(8,128)} %copy.200, pred[8,9]{1,0:T(8,128)(4,1)S(1)} %copy-done.12), kind=kLoop, calls=%fused_computation.5 | loop fusion | flops 7077888 | bytes 11796552 | tf_op jit(solution)/shard_map/jit(_where)/select_n | solution.py:75
  185.0 11.3 %convert_bitcast_fusion = f32[1,16,32,32,64]{3,1,4,2,0:T(8,128)} fusion(bf16[32,32,1,72,16]{1,4,3,0,2:T(8,128)(2,1)} %bitcast.55), kind=kLoop, calls=%fused_computation.7 | loop fusion | flops 1048576 | bytes 6291456 | tf_op jit(solution)/shard_map/reshape | solution.py:36
  196.3 30.0 %copy.201 = f32[1,16,32,32,64]{1,4,3,2,0:T(8,128)} copy(f32[1,16,32,32,64]{3,1,4,2,0:T(8,128)} %convert_bitcast_fusion) | data formatting | bytes 8388608 | tf_op jit(solution)/shard_map/reshape | solution.py:36
  226.3 25.2 %reduce_sum.9 = f32[16,16,16,32]{0,3,2,1:T(8,128)} reduce(f32[16,16,2,16,2,32,2]{0,6,5,4,3,2,1:T(2,128)} %bitcast.52, f32[]{:T(128)} %constant.5.clone.1), dimensions={2,4,6}, to_apply=%region_0.1 | reduce | flops 917504 | bytes 4718596 | tf_op jit(solution)/shard_map/reduce_sum | solution.py:37
  251.5 2.7 fusion.24
  255.5 11.7 %slice.71 = f32[32,32,1,64,16]{1,4,3,0,2:T(8,128)} slice(f32[32,32,1,72,16]{1,4,3,0,2:T(8,128)} %bitcast.54), slice={[0:32], [0:32], [0:1], [0:64], [0:16]} | slice | bytes 8388608 | tf_op jit(solution)/shard_map/jit(_where)/select_n | solution.py:75
  267.2 1.9 collective-permute-start.4
  269.0 3.8 collective-permute-start.5
  272.8 30.0 %copy.232 = f32[32,32,1,64,16]{4,3,1,0,2:T(8,128)} copy(f32[32,32,1,64,16]{1,4,3,0,2:T(8,128)} %slice.71) | data formatting | bytes 8388608
  302.8 65.2 %copy.223 = bf16[1,34,66,4,32]{3,0,2,1,4:T(2,128)(2,1)} copy(bf16[1,34,66,4,32]{2,4,3,1,0:T(8,128)(2,1)S(1)} %bitcast.67) | data formatting | bytes 1148928 | tf_op jit(solution)/shard_map/reshape | solution.py:48
  369.4 2.2 copy.216
  371.6 3.4 pad_maximum_fusion.2
  375.1 6.2 copy.234
  381.3 2.3 pad.9.clone
  383.6 5.9 copy.219
  389.5 1.6 slice.69
  391.2 7.8 convert_multiply_fusion
  401.5 16.7 %broadcast_in_dim.12 = f32[16,16,2,16,2,32,2]{0,6,5,4,3,2,1:T(2,128)} broadcast(f32[16,16,16,32]{0,3,2,1:T(8,128)S(1)} %copy.221), dimensions={0,1,3,5} | broadcast | bytes 4718592 | tf_op jit(solution)/shard_map/broadcast_in_dim | solution.py:42
  418.2 27.8 %fusion = bf16[1,16,32,32,64]{1,4,3,2,0:T(8,128)(2,1)} fusion(f32[1,16,32,32,64]{1,4,3,2,0:T(8,128)} %bitcast.53, f32[32,32,1,64,16]{4,3,1,0,2:T(8,128)} %copy.232), kind=kLoop, calls=%fused_computation.1 | loop fusion | flops 2097152 | bytes 10485760 | tf_op jit(solution)/shard_map/convert_element_type | solution.py:76
  449.1 2.4 collective-permute-start.7
  451.5 374.3 %fusion.1 = f32[16,4,3,3,3]{0,1,4,3,2:T(4,128)} fusion(bf16[1,34,66,4,32]{3,0,2,1,4:T(2,128)(2,1)} %copy.223, bf16[1,16,32,32,64]{1,4,3,2,0:T(8,128)(2,1)} %fusion), kind=kOutput, calls=%fused_computation.2 | convolution fusion | flops 221773824 | bytes 2678528 | tf_op jit(solution)/shard_map/conv_general_dilated | solution.py:25
  827.3 2.2 copy.206
  829.5 2.4 pad_maximum_fusion.1
  831.9 5.2 copy.207
  837.1 2.2 pad.7
  839.3 7.2 copy.209
  846.5 1.6 slice.65
  848.1 7.6 select_convert_fusion.1
  856.7 2.9 copy.211
  859.6 2.2 copy.228
  861.8 9.7 copy.226
  871.5 48.2 %fusion.43 = f32[16,16,3,3,3]{0,1,4,3,2:T(8,128)S(1)} fusion(bf16[1,18,34,16,16]{3,0,2,1,4:T(2,128)(2,1)} %copy.226, bf16[1,16,32,16,16]{3,0,2,1,4:T(2,128)(2,1)} %copy.227), kind=kOutput, calls=%fused_computation.59 | convolution fusion | flops 108527616 | bytes 603136 | tf_op jit(solution)/shard_map/conv_general_dilated | solution.py:25
  919.8 29.4 %all-reduce = (f32[16,4,3,3,3]{0,1,4,3,2:T(4,128)S(1)}, f32[16,16,3,3,3]{0,1,4,3,2:T(8,128)S(1)}) all-reduce(f32[16,4,3,3,3]{0,1,4,3,2:T(4,128)S(1)} %copy-done.11, f32[16,16,3,3,3]{0,1,4,3,2:T(8,128)S(1)} %fusion.43), channel_id=1, replica_groups=mesh['rep'=2,'tx'=8,'ty'=8] {'ty'}, use_global_device_ids=true, to_apply=%region_1.2 | all-reduce | flops 8640 | bytes 69120 | tf_op jit(solution)/shard_map/psum | solution.py:79
  949.2 43.0 %all-reduce.1 = (bf16[16,4,3,3,3]{0,1,4,3,2:T(4,128)(2,1)S(1)}, bf16[16,16,3,3,3]{0,1,4,3,2:T(8,128)(2,1)S(1)}) all-reduce(f32[16,4,3,3,3]{0,1,4,3,2:T(4,128)S(1)} %get-tuple-element.24, f32[16,16,3,3,3]{0,1,4,3,2:T(8,128)S(1)} %get-tuple-element.25), channel_id=1, replica_groups=mesh['rep'=2,'tx'=8,'ty'=8] {'tx'}, use_global_device_ids=true, to_apply=%region_2.3 | all-reduce | flops 8640 | bytes 51840 | tf_op jit(solution)/shard_map/psum | solution.py:79
  992.2 9.2 all-reduce.2
  (82 shorter events, 23.4 us)
Async XLA Ops:
  0.6 390.5 %copy-start = (bf16[16,16,3,3,3]{1,0,4,3,2:T(8,128)(2,1)S(1)}, bf16[16,16,3,3,3]{1,0,4,3,2:T(8,128)(2,1)}, u32[]{:S(2)}) copy-start(bf16[16,16,3,3,3]{1,0,4,3,2:T(8,128)(2,1)} %param.6) | copy-start | bytes 41476
  2.2 19.0 %collective-permute-start = (bf16[1,1,64,128]{2,3,1,0:T(8,128)(2,1)S(1)}, bf16[1,1,64,128]{2,3,1,0:T(8,128)(2,1)S(1)}, u32[]{:S(2)}, u32[]{:S(2)}) collective-permute-start(bf16[1,1,64,128]{2,3,1,0:T(8,128)(2,1)S(1)} %get-tuple-element.38), channel_id=1, source_target_pairs={{0,8},{8,16},{16,24},{24,32},{32,40},{40,48},{48,56},{56,0},{1,9},... | collective-permute-start | bytes 49160 | tf_op jit(solution)/shard_map/ppermute | solution.py:18
  5.6 15.6 %collective-permute-start.1 = (bf16[1,1,64,128]{2,3,1,0:T(8,128)(2,1)S(1)}, bf16[1,1,64,128]{2,3,1,0:T(8,128)(2,1)S(1)}, u32[]{:S(2)}, u32[]{:S(2)}) collective-permute-start(bf16[1,1,64,128]{2,3,1,0:T(8,128)(2,1)S(1)} %get-tuple-element.39), channel_id=1, source_target_pairs={{8,0},{16,8},{24,16},{32,24},{40,32},{48,40},{56,48},{0,56},{9,1},... | collective-permute-start | bytes 49160 | tf_op jit(solution)/shard_map/ppermute | solution.py:19
  8.7 17.7 %collective-permute-start.9 = (bf16[1,1,32,256]{3,2,1,0:T(8,128)(2,1)S(1)}, bf16[1,1,32,256]{3,2,1,0:T(8,128)(2,1)S(1)}, u32[]{:S(2)}, u32[]{:S(2)}) collective-permute-start(bf16[1,1,32,256]{3,2,1,0:T(8,128)(2,1)S(1)} %get-tuple-element.42), channel_id=1, source_target_pairs={{8,0},{16,8},{24,16},{32,24},{40,32},{48,40},{56,48},{0,56},{9,1},... | collective-permute-start | bytes 49160 | tf_op jit(solution)/shard_map/ppermute | solution.py:19
  12.0 9.9 collective-permute-start.8
  21.2 0.9 copy-start.7
  22.1 0.7 copy-start.8
  23.8 11.3 %collective-permute-start.3 = (bf16[1,34,1,128]{3,1,2,0:T(8,128)(2,1)S(1)}, bf16[1,34,1,128]{3,1,2,0:T(8,128)(2,1)S(1)}, u32[]{:S(2)}, u32[]{:S(2)}) collective-permute-start(bf16[1,34,1,128]{3,1,2,0:T(8,128)(2,1)S(1)} %copy.195), channel_id=1, source_target_pairs={{1,0},{2,1},{3,2},{4,3},{5,4},{6,5},{7,6},{0,7},{9,8},{10,9},{11,1... | collective-permute-start | bytes 26120 | tf_op jit(solution)/shard_map/ppermute | solution.py:19
  26.4 8.1 collective-permute-start.2
  31.5 337.9 %collective-permute-start.11 = (bf16[1,18,1,256]{3,1,2,0:T(8,128)(2,1)}, bf16[1,18,1,256]{3,1,2,0:T(8,128)(2,1)}, u32[]{:S(2)}, u32[]{:S(2)}) collective-permute-start(bf16[1,18,1,256]{3,1,2,0:T(8,128)(2,1)} %copy.231), channel_id=1, source_target_pairs={{1,0},{2,1},{3,2},{4,3},{5,4},{6,5},{7,6},{0,7},{9,8},{10,9},{11,1... | collective-permute-start | bytes 27656 | tf_op jit(solution)/shard_map/ppermute | solution.py:19
  34.5 333.5 %collective-permute-start.10 = (bf16[1,18,1,256]{3,1,2,0:T(8,128)(2,1)}, bf16[1,18,1,256]{3,1,2,0:T(8,128)(2,1)}, u32[]{:S(2)}, u32[]{:S(2)}) collective-permute-start(bf16[1,18,1,256]{3,1,2,0:T(8,128)(2,1)} %copy.230), channel_id=1, source_target_pairs={{0,1},{1,2},{2,3},{3,4},{4,5},{5,6},{6,7},{7,0},{8,9},{9,10},{10,1... | collective-permute-start | bytes 27656 | tf_op jit(solution)/shard_map/ppermute | solution.py:18
  39.0 4.8 copy-start.4
  44.6 15.7 %copy-start.13 = (bf16[16,4,3,3,3]{0,1,4,3,2:T(4,128)(2,1)S(1)}, bf16[16,4,3,3,3]{0,1,4,3,2:T(4,128)(2,1)}, u32[]{:S(2)}) copy-start(bf16[16,4,3,3,3]{0,1,4,3,2:T(4,128)(2,1)} %param.5) | copy-start | bytes 10372
  139.6 27.7 %copy-start.12 = (pred[8,9]{1,0:T(8,128)(4,1)S(1)}, pred[8,9]{1,0:T(8,128)(4,1)}, u32[]{:S(2)}) copy-start(pred[8,9]{1,0:T(8,128)(4,1)} %constant.34) | copy-start | bytes 220
  255.4 11.7 %copy-start.1 = (bf16[1,16,32,16,16]{2,4,3,1,0:T(8,128)(2,1)}, bf16[1,16,32,16,16]{2,4,3,1,0:T(8,128)(2,1)S(1)}, u32[]{:S(2)}) copy-start(bf16[1,16,32,16,16]{2,4,3,1,0:T(8,128)(2,1)S(1)} %copy.202) | copy-start | bytes 786436
  267.2 178.8 %collective-permute-start.4 = (bf16[1,1,32,256]{2,3,1,0:T(8,128)(2,1)S(1)}, bf16[1,1,32,256]{2,3,1,0:T(8,128)(2,1)S(1)}, u32[]{:S(2)}, u32[]{:S(2)}) collective-permute-start(bf16[1,1,32,256]{2,3,1,0:T(8,128)(2,1)S(1)} %get-tuple-element.36), channel_id=1, source_target_pairs={{0,8},{8,16},{16,24},{24,32},{32,40},{40,48},{48,56},{56,0},{1,9},... | collective-permute-start | bytes 49160 | tf_op jit(solution)/shard_map/ppermute | solution.py:18
  269.0 33.8 %copy-start.5 = (bf16[1,34,66,128]{2,3,1,0:T(8,128)(2,1)S(1)}, bf16[1,34,66,128]{2,3,1,0:T(8,128)(2,1)}, u32[]{:S(2)}) copy-start(bf16[1,34,66,128]{2,3,1,0:T(8,128)(2,1)} %copy-done.4) | copy-start | bytes 1723396
  269.0 176.9 %collective-permute-start.5 = (bf16[1,1,32,256]{2,3,1,0:T(8,128)(2,1)S(1)}, bf16[1,1,32,256]{2,3,1,0:T(8,128)(2,1)S(1)}, u32[]{:S(2)}, u32[]{:S(2)}) collective-permute-start(bf16[1,1,32,256]{2,3,1,0:T(8,128)(2,1)S(1)} %get-tuple-element.37), channel_id=1, source_target_pairs={{8,0},{16,8},{24,16},{32,24},{40,32},{48,40},{56,48},{0,56},{9,1},... | collective-permute-start | bytes 49160 | tf_op jit(solution)/shard_map/ppermute | solution.py:19
  368.0 3.6 copy-start.6
  383.6 7.6 copy-start.14
  418.1 27.8 %copy-start.2 = (bf16[1,16,32,16,16]{2,4,3,1,0:T(8,128)(2,1)S(1)}, bf16[1,16,32,16,16]{2,4,3,1,0:T(8,128)(2,1)}, u32[]{:S(2)}) copy-start(bf16[1,16,32,16,16]{2,4,3,1,0:T(8,128)(2,1)} %copy-done.1) | copy-start | bytes 786436
  445.9 0.8 copy-start.9
  445.9 0.8 copy-start.10
  449.1 378.2 %collective-permute-start.7 = (bf16[1,18,1,256]{3,1,2,0:T(8,128)(2,1)}, bf16[1,18,1,256]{3,1,2,0:T(8,128)(2,1)}, u32[]{:S(2)}, u32[]{:S(2)}) collective-permute-start(bf16[1,18,1,256]{3,1,2,0:T(8,128)(2,1)} %copy.204), channel_id=1, source_target_pairs={{1,0},{2,1},{3,2},{4,3},{5,4},{6,5},{7,6},{0,7},{9,8},{10,9},{11,1... | collective-permute-start | bytes 27656 | tf_op jit(solution)/shard_map/ppermute | solution.py:19
  451.5 374.3 %collective-permute-start.6 = (bf16[1,18,1,256]{3,1,2,0:T(8,128)(2,1)}, bf16[1,18,1,256]{3,1,2,0:T(8,128)(2,1)}, u32[]{:S(2)}, u32[]{:S(2)}) collective-permute-start(bf16[1,18,1,256]{3,1,2,0:T(8,128)(2,1)} %copy.203), channel_id=1, source_target_pairs={{0,1},{1,2},{2,3},{3,4},{4,5},{5,6},{6,7},{7,0},{8,9},{9,10},{10,1... | collective-permute-start | bytes 27656 | tf_op jit(solution)/shard_map/ppermute | solution.py:18
  825.8 3.7 copy-start.3
  839.3 8.9 copy-start.15
  871.5 48.2 %copy-start.11 = (f32[16,4,3,3,3]{0,1,4,3,2:T(4,128)S(1)}, f32[16,4,3,3,3]{0,1,4,3,2:T(4,128)}, u32[]{:S(2)}) copy-start(f32[16,4,3,3,3]{0,1,4,3,2:T(4,128)} %fusion.1) | copy-start | bytes 20740
